TPU v7x, 256 devices: a whole 4x4x8 slice. The times are simulated.
256 devices in a mesh: ent: 32 (over y, x, core), rel: 8 (over z).
Axes of the slice: x: 4, y: 4, z: 8, core: 2. Of those that a mesh axis runs over, the one named last changes fastest.
Arguments:
- tile_vals: bfloat16 [32, 8, 64, 128, 128], P('ent', 'rel'), may hold values from -192 to 192
- tile_row: int32 [32, 8, 64], P('ent', 'rel'), may hold values from 0 to 3
- tile_rel: int32 [32, 8, 64], P('ent', 'rel'), may hold values from 0 to 1
- tile_src: int32 [32, 8, 64], P('ent', 'rel'), may hold values from 0 to 31
- needed: int32 [32, 8, 32, 1], P('ent', 'rel'), may hold values from 0 to 3
- factors: bfloat16 [16384, 256], P('ent'), may hold values from -6 to 6
- cores: bfloat16 [16, 256, 256], P('rel'), may hold values from -0.5 to 1.5
- basis: float32 [256, 256], replicated, may hold values from -1 to 1
- spectrum: float32 [256], replicated, may hold values from 100 to 1000
Outputs:
- new_factors: bfloat16 [16384, 256], P('ent')
- new_cores: float32 [16, 256, 256], P('rel')
Inputs may be any that keep to these rules, and one draw needn't show every extreme that they name: tile_src names the owner whose single requested block (slot 0 of `needed`) gives the tile's columns. `needed`: every request slot names a block.
All inputs are finite; a program needn't handle non-finite values.
Results may differ from a plain program's by a relative error of at most 0.0081.
Values may be sent and summed in bfloat16 or wider, within the bound.
A program may use at most 64 MiB of HBM per device.

v0:
```python
import jax
import jax.numpy as jnp
from jax import lax
from jax.sharding import PartitionSpec as P

ridge_shift = 1.0


def shards(tile_vals, tile_row, tile_rel, tile_src, needed, factors, cores, basis, spectrum):
    precise = lax.Precision.HIGHEST
    tile_data = tile_vals[0, 0]
    tile_rows = tile_row[0, 0]
    tile_rels = tile_rel[0, 0]
    sources = tile_src[0, 0]
    asked_rows = needed[0, 0]
    count_ent, slot_count = asked_rows.shape
    tile_edge = tile_data.shape[1]
    rank_width = factors.shape[1]
    rel_local = cores.shape[0]
    row_blocks = factors.shape[0] // tile_edge
    slot_total = count_ent * slot_count
    requests = lax.all_to_all(asked_rows, "ent", split_axis=0, concat_axis=0, tiled=True)

    def neighbour(slab_rows):
        whole_table = lax.all_gather(slab_rows, "ent", axis=0, tiled=True).reshape(
            count_ent, row_blocks, tile_edge, rank_width
        )
        fetched = whole_table[jnp.arange(count_ent)[:, None], asked_rows]
        return fetched.reshape(slot_total, tile_edge, rank_width)[sources]

    def grouped(part_data, key_ids, group_count):
        onehot = (key_ids[:, None] == jnp.arange(group_count, dtype=jnp.int32)[None, :]).astype(
            jnp.bfloat16
        )
        flat_part = part_data.reshape(part_data.shape[0], tile_edge * rank_width)
        return jnp.einsum(
            "tg,tx->gx", onehot, flat_part, preferred_element_type=jnp.float32
        ).astype(jnp.bfloat16)

    gathered_old = neighbour(factors)
    left_part = jnp.einsum(
        "tab,tbr->tar", tile_data, gathered_old, preferred_element_type=jnp.float32
    ).astype(jnp.bfloat16)
    forward = grouped(
        left_part, tile_rels * row_blocks + tile_rows, rel_local * row_blocks
    ).reshape(rel_local, row_blocks, tile_edge, rank_width)
    forward_term = jnp.einsum(
        "kbar,ksr->bas", forward, cores, preferred_element_type=jnp.float32
    ).reshape(-1, rank_width)
    own_blocks = factors.reshape(row_blocks, tile_edge, rank_width)
    right_part = jnp.einsum(
        "tab,tar->tbr", tile_data, own_blocks[tile_rows], preferred_element_type=jnp.float32
    ).astype(jnp.bfloat16)
    backward = grouped(right_part, sources * rel_local + tile_rels, slot_total * rel_local).reshape(
        slot_total, rel_local, tile_edge, rank_width
    )
    backward_term = jnp.einsum(
        "skbr,krq->sbq", backward, cores, preferred_element_type=jnp.float32
    ).reshape(count_ent, slot_count, tile_edge, rank_width)
    returned = lax.all_to_all(backward_term, "ent", split_axis=0, concat_axis=0, tiled=True)
    landing = (
        requests.reshape(1, slot_total) == jnp.arange(row_blocks, dtype=jnp.int32)[:, None]
    ).astype(jnp.float32)
    landed = jnp.dot(
        landing,
        returned.reshape(slot_total, tile_edge * rank_width),
        precision=precise,
        preferred_element_type=jnp.float32,
    ).reshape(-1, rank_width)
    gram_total = lax.psum(
        jnp.einsum("ar,as->rs", factors, factors, preferred_element_type=jnp.float32), "ent"
    )
    core_f32 = cores.astype(jnp.float32)
    system_part = jnp.einsum("kab,bc,kdc->ad", core_f32, gram_total, core_f32, precision=precise)
    system_part = system_part + jnp.einsum(
        "kba,bc,kcd->ad", core_f32, gram_total, core_f32, precision=precise
    )
    numerator, system = lax.psum((forward_term + landed, system_part), "rel")
    system = system + ridge_shift * jnp.eye(rank_width, dtype=jnp.float32)
    factor_low = jnp.linalg.cholesky(system)
    new_factors = jax.scipy.linalg.cho_solve((factor_low, True), numerator.T).T.astype(jnp.bfloat16)
    gathered_new = neighbour(new_factors)
    latest = jnp.einsum(
        "tab,tbr->tar", tile_data, gathered_new, preferred_element_type=jnp.float32
    ).astype(jnp.bfloat16)
    summed = grouped(latest, tile_rels * row_blocks + tile_rows, rel_local * row_blocks).reshape(
        rel_local, row_blocks, tile_edge, rank_width
    )
    core_part = jnp.einsum(
        "bar,kbas->krs",
        new_factors.reshape(row_blocks, tile_edge, rank_width),
        summed,
        preferred_element_type=jnp.float32,
    )
    weights = 1.0 / (spectrum[:, None] * spectrum[None, :] + ridge_shift)
    totals = lax.psum(core_part, "ent")
    rotated = jnp.einsum("ri,krs,sj->kij", basis, totals, basis, precision=precise)
    new_cores = jnp.einsum(
        "ir,krs,js->kij", basis, weights[None] * rotated, basis, precision=precise
    )
    return (new_factors, new_cores)


def solution(mesh):
    in_specs = (
        P("ent", "rel", None, None, None),
        P("ent", "rel", None),
        P("ent", "rel", None),
        P("ent", "rel", None),
        P("ent", "rel", None, None),
        P("ent", None),
        P("rel", None, None),
        P(),
        P(),
    )
    out_specs = (P("ent", None), P("rel", None, None))
    return jax.shard_map(shards, mesh=mesh, in_specs=in_specs, out_specs=out_specs, check_vma=False)
```

profile of v0, /device:TPU:1, one launch (start us, length us, event | category | flops | bytes accessed | tf_op | source)
XLA Modules:
  0.0 606.0 jit_solution(6752421999504624473)
XLA Ops:
  11.5 8.6 %all-to-all-start = ((s32[32,1,1]{2,1,0:T(1,128)}), s32[32,1,1]{2,1,0:T(1,128)S(1)}, u32[]{:S(2)}, u32[]{:S(2)}) async-start(s32[32,1,1]{2,1,0:T(1,128)} %copy.58), calls=%async_computation | async-start | bytes 32768 | tf_op jit(solution)/shard_map/all_to_all | solution.py:22
  23.5 5.5 convert_bitcast_fusion.1
  29.0 6.8 %copy.96 = bf16[8,8,128,256]{3,1,2,0:T(8,128)(2,1)} copy(bf16[8,8,128,256]{2,3,1,0:T(8,128)(2,1)} %bitcast.176) | data formatting | bytes 8388608
  43.8 7.6 %all-to-all-start.1 = ((f32[32,1,128,256]{3,2,1,0:T(8,128)}), f32[32,1,128,256]{3,2,1,0:T(8,128)}, u32[]{:S(2)}, u32[]{:S(2)}) async-start(f32[32,1,128,256]{3,2,1,0:T(8,128)} %convolution_bitcast_fusion), calls=%async_computation.1 | async-start | bytes 8388608 | tf_op jit(solution)/shard_map/all_to_all | solution.py:60
  52.6 100.5 %all-reduce.6.cloned.1.call-done = f32[256,256]{1,0:T(8,128)} async-done(((f32[256,256]{1,0:T(8,128)}), f32[256,256]{1,0:T(8,128)}) %all-reduce.6.cloned.1.call-update) | async-done | bytes 262160 | tf_op jit(solution)/shard_map/psum | solution.py:70
  157.5 4.6 copy.98
  164.1 50.2 %all-gather.3.cloned.1.call-done = bf16[16384,256]{1,0:T(8,128)(2,1)} async-done(((bf16[512,256]{1,0:T(8,128)(2,1)}), bf16[16384,256]{1,0:T(8,128)(2,1)}) %all-gather.3.cloned.1.call-update) | async-done | bytes 8388624 | tf_op jit(solution)/shard_map/all_gather | solution.py:25
  214.2 5.4 gather_fusion
  219.7 4.4 gather_fusion.1
  224.0 5.5 convert_bitcast_fusion.2
  229.5 6.8 %copy.94 = bf16[8,8,128,256]{3,1,2,0:T(8,128)(2,1)} copy(bf16[8,8,128,256]{2,3,1,0:T(8,128)(2,1)} %bitcast.177) | data formatting | bytes 8388608
  240.8 69.7 %all-reduce.10.cloned.1.call-done = (f32[256,512]{0,1:T(8,128)}, f32[256,256]{0,1:T(8,128)}) async-done(((f32[256,512]{0,1:T(8,128)}, f32[256,256]{0,1:T(8,128)}), (f32[256,512]{0,1:T(8,128)}, f32[256,256]{0,1:T(8,128)})) %all-reduce.10.cloned.1.call-update) | async-done | bytes 786448 | tf_op jit(solution)/shard_map/psum | solution.py:78
  312.7 11.7 %cholesky.50 = f32[128,128]{1,0:T(8,128)S(1)} custom-call(f32[128,128]{1,0:T(8,128)S(1)} %cholesky.118), custom_call_target="Cholesky" | custom-call | tf_op jit(solution)/shard_map/jit(cholesky)/cholesky | solution.py:80
  324.4 9.8 %custom-call.18 = f32[1,128,128]{1,2,0:T(8,128)S(1)} custom-call(f32[1,128,128]{2,1,0:T(8,128)S(1)} %get-tuple-element.33), custom_call_target="InvertDiagBlocksLowerTriangular" | custom-call | tf_op jit(solution)/shard_map/jit(cholesky)/cholesky | solution.py:80
  334.7 11.7 %cholesky.105 = f32[128,128]{1,0:T(8,128)S(1)} custom-call(f32[128,128]{1,0:T(8,128)S(1)} %convolution_subtract_fusion.2), custom_call_target="Cholesky" | custom-call | tf_op jit(solution)/shard_map/jit(cholesky)/cholesky | solution.py:80
  348.5 4.2 while.1
  352.7 19.7 %custom-call.19 = f32[2,128,128]{1,2,0:T(8,128)S(1)} custom-call(f32[2,128,128]{2,1,0:T(8,128)S(1)} %get-tuple-element.9), custom_call_target="InvertDiagBlocksLowerTriangular" | custom-call | tf_op jit(solution)/shard_map/jit(_cho_solve)/triangular_solve | solution.py:81
  376.9 66.5 %all-gather.5.cloned.1.call-done = bf16[16384,256]{0,1:T(8,128)(2,1)} async-done(((bf16[512,256]{0,1:T(8,128)(2,1)}), bf16[16384,256]{0,1:T(8,128)(2,1)}) %all-gather.5.cloned.1.call-update) | async-done | bytes 8388624 | tf_op jit(solution)/shard_map/all_gather | solution.py:25
  443.4 12.0 %copy.92 = bf16[16384,256]{1,0:T(8,128)(2,1)} copy(bf16[16384,256]{0,1:T(8,128)(2,1)} %all-gather.5.cloned.1.call-done) | data formatting | bytes 16777216 | tf_op jit(solution)/shard_map/reshape | solution.py:25
  455.4 5.4 gather_fusion.3
  460.8 4.4 gather_fusion.4
  465.2 5.5 convert_bitcast_fusion
  470.7 6.8 %copy.99 = bf16[8,8,128,256]{3,1,2,0:T(8,128)(2,1)} copy(bf16[8,8,128,256]{2,3,1,0:T(8,128)(2,1)} %bitcast.178) | data formatting | bytes 8388608
  481.9 112.9 %all-reduce.8.cloned.1.call-done = f32[2,256,256]{1,2,0:T(8,128)} async-done(((f32[2,256,256]{1,2,0:T(8,128)}), f32[2,256,256]{1,2,0:T(8,128)}) %all-reduce.8.cloned.1.call-update) | async-done | bytes 524304 | tf_op jit(solution)/shard_map/psum | solution.py:96
  (95 shorter events, 48.1 us)
Async XLA Ops:
  7.2 16.4 %copy-start = (bf16[1,1,64,128,128]{4,3,2,1,0:T(8,128)(2,1)S(1)}, bf16[1,1,64,128,128]{4,3,2,1,0:T(8,128)(2,1)}, u32[]{:S(2)}) copy-start(bf16[1,1,64,128,128]{4,3,2,1,0:T(8,128)(2,1)} %param.9) | copy-start | bytes 6291460
  7.2 13.6 %copy-start.1 = (bf16[512,256]{1,0:T(8,128)(2,1)S(1)}, bf16[512,256]{1,0:T(8,128)(2,1)}, u32[]{:S(2)}) copy-start(bf16[512,256]{1,0:T(8,128)(2,1)} %param.14) | copy-start | bytes 786436
  7.2 145.9 %all-reduce.6.cloned.1.call-start = ((), (), s32[]{:S(2)}) async-start(), calls=%async_computation.2 | async-start | bytes 524288 | tf_op jit(solution)/shard_map/psum | solution.py:70
  9.4 204.8 %all-gather.3.cloned.1.call-start = ((), (), s32[]{:S(2)}) async-start(), calls=%async_computation.3 | async-start | bytes 8650752 | tf_op jit(solution)/shard_map/all_gather | solution.py:25
  11.5 32.2 %all-to-all-start = ((s32[32,1,1]{2,1,0:T(1,128)}), s32[32,1,1]{2,1,0:T(1,128)S(1)}, u32[]{:S(2)}, u32[]{:S(2)}) async-start(s32[32,1,1]{2,1,0:T(1,128)} %copy.58), calls=%async_computation | async-start | bytes 32768 | tf_op jit(solution)/shard_map/all_to_all | solution.py:22
  29.0 6.8 %copy-start.7 = (s32[1,1,64]{2,1,0:T(1,128)S(1)}, s32[1,1,64]{2,1,0:T(1,128)}, u32[]{:S(2)}) copy-start(s32[1,1,64]{2,1,0:T(1,128)} %param.10) | copy-start | bytes 772
  29.0 6.8 %copy-start.8 = (s32[1,1,64]{2,1,0:T(1,128)S(1)}, s32[1,1,64]{2,1,0:T(1,128)}, u32[]{:S(2)}) copy-start(s32[1,1,64]{2,1,0:T(1,128)} %param.11) | copy-start | bytes 772
  29.0 6.8 %copy-start.10 = (s32[1,1,64]{2,1,0:T(1,128)S(1)}, s32[1,1,64]{2,1,0:T(1,128)}, u32[]{:S(2)}) copy-start(s32[1,1,64]{2,1,0:T(1,128)} %param.12) | copy-start | bytes 772
  39.4 1.1 copy-start.2
  43.8 8.1 %copy-start.9 = (s32[1,1,32,1]{2,3,1,0:T(1,128)S(1)}, s32[1,1,32,1]{2,3,1,0:T(1,128)}, u32[]{:S(2)}) copy-start(s32[1,1,32,1]{2,3,1,0:T(1,128)} %param.13) | copy-start | bytes 388
  43.8 113.8 %all-to-all-start.1 = ((f32[32,1,128,256]{3,2,1,0:T(8,128)}), f32[32,1,128,256]{3,2,1,0:T(8,128)}, u32[]{:S(2)}, u32[]{:S(2)}) async-start(f32[32,1,128,256]{3,2,1,0:T(8,128)} %convolution_bitcast_fusion), calls=%async_computation.1 | async-start | bytes 8388608 | tf_op jit(solution)/shard_map/all_to_all | solution.py:60
  51.3 259.1 %all-reduce.10.cloned.1.call-start = ((), (), s32[]{:S(2)}) async-start(), calls=%async_computation.6 | async-start | bytes 1572864 | tf_op jit(solution)/shard_map/psum | solution.py:78
  240.5 202.9 %all-gather.5.cloned.1.call-start = ((), (), s32[]{:S(2)}) async-start(), calls=%async_computation.4 | async-start | bytes 8650752 | tf_op jit(solution)/shard_map/all_gather | solution.py:25
  310.5 61.9 %copy-start.5 = (f32[256,512]{0,1:T(8,128)S(1)}, f32[256,512]{0,1:T(8,128)}, u32[]{:S(2)}) copy-start(f32[256,512]{0,1:T(8,128)} %get-tuple-element.26) | copy-start | bytes 1572868
  375.8 219.1 %all-reduce.8.cloned.1.call-start = ((), (), s32[]{:S(2)}) async-start(), calls=%async_computation.5 | async-start | bytes 1048576 | tf_op jit(solution)/shard_map/psum | solution.py:96
  376.9 103.7 %copy-start.4 = (bf16[512,256]{1,0:T(8,128)(2,1)}, bf16[512,256]{1,0:T(8,128)(2,1)S(1)}, u32[]{:S(2)}) copy-start(bf16[512,256]{1,0:T(8,128)(2,1)S(1)} %copy.71) | copy-start | bytes 786436
  477.5 4.3 copy-start.6
  477.5 117.4 %copy-start.3 = (f32[256,256]{1,0:T(8,128)S(1)}, f32[256,256]{1,0:T(8,128)}, u32[]{:S(2)}) copy-start(f32[256,256]{1,0:T(8,128)} %param.16) | copy-start | bytes 786436
Sparse Core Ops, SparseCore 0:
  11.8 141.2 all-reduce.5
  156.0 58.1 all-gather.2
  240.7 69.7 all-reduce.9
  375.9 67.4 all-gather.4
  481.9 112.9 all-reduce.7
where the time goes:
time: 613 us; the launch traced here: 606 us
  waiting for transfers between devices  401 us (65%)
  local copies, waits for them, and re-layouts  67.8 us (11%)
  other arithmetic  57.9 us (9%)
  matrix products  46.8 us (8%)
  starting transfers between devices  17 us (3%)
  between operations  15.7 us (3%)
    all_gather x2, waiting for transfers between devices, neighbour(): lax.all_gather(slab_rows, 'ent', axis=0, tiled=True)  117 us
    psum x1, waiting for transfers between devices, shards(): totals = lax.psum(core_part, 'ent')  113 us
    psum x1, waiting for transfers between devices, shards(): lax.psum(jnp.einsum('ar,as->rs', factors, factors, preferred_element_type...  101 us
    psum x1, waiting for transfers between devices, shards(): numerator, system = lax.psum((forward_term + landed, system_part), 'rel')  69.7 us
    another operation x6, other arithmetic, shards(): factor_low = jnp.linalg.cholesky(system)  34 us
    unnamed x30, local copies, waits for them, and re-layouts  27.6 us
    another operation x3, other arithmetic, shards(): jax.scipy.linalg.cho_solve((factor_low, True), numerator.T)  19.7 us
  transfers between devices with their start and end apart: 7, of which 5 were waited for; matrix products, arithmetic and copies ran while one was open for 6% of the time, Pallas kernels for 0%

commit v1 on v0

--- a/solution.py
+++ b/solution.py
@@ -22,7 +22,14 @@
     requests = lax.all_to_all(asked_rows, "ent", split_axis=0, concat_axis=0, tiled=True)
 
     def neighbour(slab_rows):
-        whole_table = lax.all_gather(slab_rows, "ent", axis=0, tiled=True).reshape(
+
+        def take_loops_on_mesh(z_in):
+            return jnp.concatenate(
+                jax.lax.all_to_all(jnp.stack(jax.lax.axis_size("ent") * [z_in]), "ent", 0, 0),
+                axis=0,
+            )
+
+        whole_table = take_loops_on_mesh(slab_rows).reshape(
             count_ent, row_blocks, tile_edge, rank_width
         )
         fetched = whole_table[jnp.arange(count_ent)[:, None], asked_rows]

time: 613 us -> 724 us (1.18)
  blocking collectives: 0 us -> 166 us
  waiting for transfers between devices: 401 us -> 357 us
  local copies, waits for them, and re-layouts: 67.8 us -> 59.9 us
    all_to_all x0 -> x2, blocking collectives: none -> 166 us  [the longest x1 107 us: take_loops_on_mesh(): jax.lax.all_to_all(jnp.stack(jax.lax.axis_size('ent') * [z_in]), 'ent', 0...]
    all_gather x2 -> x0, waiting for transfers between devices: 117 us -> none  [neighbour(): lax.all_gather(slab_rows, 'ent', axis=0, tiled=True)]
    psum x1, waiting for transfers between devices: 101 us -> 177 us  [shards(): lax.psum(jnp.einsum('ar,as->rs', factors, factors, preferred_element_type...]
    reshape x1 -> x0, local copies, waits for them, and re-layouts: 12 us -> none  [neighbour(): lax.all_gather(slab_rows, 'ent', axis=0, tiled=True)]
    unnamed x30 -> x32, local copies, waits for them, and re-layouts: 27.6 us -> 24.4 us
  transfers between devices with their start and end apart: 7 -> 5, of which waited for: 5 -> 3; matrix products, arithmetic and copies ran while one was open for 6% -> 5% of each run, Pallas kernels for 0% -> 0%
where the time goes in v1:
time: 724 us; the launch traced here: 717 us
  waiting for transfers between devices  357 us (49%)
  blocking collectives  166 us (23%)
  local copies, waits for them, and re-layouts  59.9 us (8%)
  other arithmetic  57.2 us (8%)
  matrix products  46.5 us (6%)
  between operations  15.7 us (2%)
  starting transfers between devices  14.4 us (2%)
    psum x1, waiting for transfers between devices, shards(): lax.psum(jnp.einsum('ar,as->rs', factors, factors, preferred_element_type...  177 us
    psum x1, waiting for transfers between devices, shards(): totals = lax.psum(core_part, 'ent')  109 us
    all_to_all x1, blocking collectives, take_loops_on_mesh(): jax.lax.all_to_all(jnp.stack(jax.lax.axis_size('ent') * [z_in]), 'ent', 0...  107 us
    psum x1, waiting for transfers between devices, shards(): numerator, system = lax.psum((forward_term + landed, system_part), 'rel')  70.3 us
    all_to_all x1, blocking collectives, shards(): lax.all_to_all(backward_term, 'ent', split_axis=0, concat_axis=0, tiled=T...  58.5 us
    another operation x6, other arithmetic, shards(): factor_low = jnp.linalg.cholesky(system)  34 us
    unnamed x32, local copies, waits for them, and re-layouts  24.4 us
    another operation x3, other arithmetic, shards(): jax.scipy.linalg.cho_solve((factor_low, True), numerator.T)  19.7 us
  transfers between devices with their start and end apart: 5, of which 3 were waited for; matrix products, arithmetic and copies ran while one was open for 5% of the time, Pallas kernels for 0%

profile of v1, /device:TPU:1, one launch (start us, length us, event | category | flops | bytes accessed | tf_op | source)
XLA Modules:
  0.0 716.9 jit_solution(9785757245316188803)
XLA Ops:
  8.7 8.6 %all-to-all-start.1 = ((s32[32,1,1]{2,1,0:T(1,128)}), s32[32,1,1]{2,1,0:T(1,128)S(1)}, u32[]{:S(2)}, u32[]{:S(2)}) async-start(s32[32,1,1]{2,1,0:T(1,128)} %copy.59), calls=%async_computation.1 | async-start | bytes 32768 | tf_op jit(solution)/shard_map/all_to_all | solution.py:22
  17.9 3.7 gather_fusion.2
  21.7 5.4 convert_bitcast_fusion.1
  27.1 6.8 copy.96
  41.9 58.5 %all_to_all.21 = f32[32,1,128,256]{3,2,1,0:T(8,128)} all-to-all(f32[32,1,128,256]{3,2,1,0:T(8,128)} %convolution_bitcast_fusion), channel_id=1, replica_groups=mesh['ent'=32,'rel'=8] {'ent'}, dimensions={0} | all-to-all | bytes 8388608 | tf_op jit(solution)/shard_map/all_to_all | solution.py:67
  100.4 4.2 stack.4
  104.6 5.1 all-to-all-start
  112.0 177.4 %all-reduce.6.cloned.1.call-done = f32[256,256]{1,0:T(8,128)} async-done(((f32[256,256]{1,0:T(8,128)}), f32[256,256]{1,0:T(8,128)}) %all-reduce.6.cloned.1.call-update) | async-done | bytes 262160 | tf_op jit(solution)/shard_map/psum | solution.py:77
  300.1 5.4 gather_fusion
  305.5 4.4 gather_fusion.1
  309.9 5.5 convert_bitcast_fusion.2
  315.3 6.8 copy.94
  326.6 70.3 %all-reduce.10.cloned.1.call-done = (f32[256,512]{0,1:T(8,128)}, f32[256,256]{0,1:T(8,128)}) async-done(((f32[256,512]{0,1:T(8,128)}, f32[256,256]{0,1:T(8,128)}), (f32[256,512]{0,1:T(8,128)}, f32[256,256]{0,1:T(8,128)})) %all-reduce.10.cloned.1.call-update) | async-done | bytes 786448 | tf_op jit(solution)/shard_map/psum | solution.py:85
  399.1 11.7 %cholesky.50 = f32[128,128]{1,0:T(8,128)S(1)} custom-call(f32[128,128]{1,0:T(8,128)S(1)} %cholesky.118), custom_call_target="Cholesky" | custom-call | tf_op jit(solution)/shard_map/jit(cholesky)/cholesky | solution.py:87
  410.8 9.8 %custom-call.18 = f32[1,128,128]{1,2,0:T(8,128)S(1)} custom-call(f32[1,128,128]{2,1,0:T(8,128)S(1)} %get-tuple-element.33), custom_call_target="InvertDiagBlocksLowerTriangular" | custom-call | tf_op jit(solution)/shard_map/jit(cholesky)/cholesky | solution.py:87
  421.1 11.7 %cholesky.105 = f32[128,128]{1,0:T(8,128)S(1)} custom-call(f32[128,128]{1,0:T(8,128)S(1)} %convolution_subtract_fusion.2), custom_call_target="Cholesky" | custom-call | tf_op jit(solution)/shard_map/jit(cholesky)/cholesky | solution.py:87
  434.9 4.2 while.1
  439.1 19.7 %custom-call.19 = f32[2,128,128]{1,2,0:T(8,128)S(1)} custom-call(f32[2,128,128]{2,1,0:T(8,128)S(1)} %get-tuple-element.9), custom_call_target="InvertDiagBlocksLowerTriangular" | custom-call | tf_op jit(solution)/shard_map/jit(_cho_solve)/triangular_solve | solution.py:88
  462.6 107.4 %all_to_all.22 = bf16[32,512,256]{2,1,0:T(8,128)(2,1)} all-to-all(bf16[32,512,256]{2,1,0:T(8,128)(2,1)S(1)} %stack.5), channel_id=1, replica_groups=mesh['ent'=32,'rel'=8] {'ent'}, dimensions={0} | all-to-all | bytes 16777216 | tf_op jit(solution)/shard_map/all_to_all | solution.py:28
  569.9 5.4 gather_fusion.3
  575.4 4.4 gather_fusion.4
  579.7 5.5 convert_bitcast_fusion
  585.2 6.8 copy.99
  596.4 109.4 %all-reduce.8.cloned.1.call-done = f32[2,256,256]{1,2,0:T(8,128)} async-done(((f32[2,256,256]{1,2,0:T(8,128)}), f32[2,256,256]{1,2,0:T(8,128)}) %all-reduce.8.cloned.1.call-update) | async-done | bytes 524304 | tf_op jit(solution)/shard_map/psum | solution.py:103
  (94 shorter events, 47.2 us)
Async XLA Ops:
  7.2 14.5 %copy-start = (bf16[1,1,64,128,128]{4,3,2,1,0:T(8,128)(2,1)S(1)}, bf16[1,1,64,128,128]{4,3,2,1,0:T(8,128)(2,1)}, u32[]{:S(2)}) copy-start(bf16[1,1,64,128,128]{4,3,2,1,0:T(8,128)(2,1)} %param.9) | copy-start | bytes 6291460
  8.7 33.2 %all-to-all-start.1 = ((s32[32,1,1]{2,1,0:T(1,128)}), s32[32,1,1]{2,1,0:T(1,128)S(1)}, u32[]{:S(2)}, u32[]{:S(2)}) async-start(s32[32,1,1]{2,1,0:T(1,128)} %copy.59), calls=%async_computation.1 | async-start | bytes 32768 | tf_op jit(solution)/shard_map/all_to_all | solution.py:22
  27.1 6.9 copy-start.8
  27.1 6.9 copy-start.9
  27.1 6.9 copy-start.11
  37.5 1.1 copy-start.3
  41.9 58.5 %copy-start.1 = (bf16[512,256]{1,0:T(8,128)(2,1)S(1)}, bf16[512,256]{1,0:T(8,128)(2,1)}, u32[]{:S(2)}) copy-start(bf16[512,256]{1,0:T(8,128)(2,1)} %param.14) | copy-start | bytes 786436
  104.6 6.6 copy-start.10
  104.6 195.5 %all-to-all-start = ((bf16[32,512,256]{2,1,0:T(8,128)(2,1)}), bf16[32,512,256]{2,1,0:T(8,128)(2,1)}, u32[]{:S(2)}, u32[]{:S(2)}) async-start(bf16[32,512,256]{2,1,0:T(8,128)(2,1)} %stack.4), calls=%async_computation | async-start | bytes 16777216 | tf_op jit(solution)/shard_map/all_to_all | solution.py:28
  109.7 179.7 %all-reduce.6.cloned.1.call-start = ((), (), s32[]{:S(2)}) async-start(), calls=%async_computation.4 | async-start | bytes 524288 | tf_op jit(solution)/shard_map/psum | solution.py:77
  110.7 286.2 %all-reduce.10.cloned.1.call-start = ((), (), s32[]{:S(2)}) async-start(), calls=%async_computation.6 | async-start | bytes 1572864 | tf_op jit(solution)/shard_map/psum | solution.py:85
  289.3 4.6 copy-start.2
  326.4 379.4 %all-reduce.8.cloned.1.call-start = ((), (), s32[]{:S(2)}) async-start(), calls=%async_computation.5 | async-start | bytes 1048576 | tf_op jit(solution)/shard_map/psum | solution.py:103
  396.9 61.9 %copy-start.6 = (f32[256,512]{0,1:T(8,128)S(1)}, f32[256,512]{0,1:T(8,128)}, u32[]{:S(2)}) copy-start(f32[256,512]{0,1:T(8,128)} %get-tuple-element.26) | copy-start | bytes 1572868
  461.6 133.5 %copy-start.5 = (bf16[512,256]{1,0:T(8,128)(2,1)}, bf16[512,256]{1,0:T(8,128)(2,1)S(1)}, u32[]{:S(2)}) copy-start(bf16[512,256]{1,0:T(8,128)(2,1)S(1)} %copy.72) | copy-start | bytes 786436
  592.0 4.3 copy-start.7
  592.0 113.8 %copy-start.4 = (f32[256,256]{1,0:T(8,128)S(1)}, f32[256,256]{1,0:T(8,128)}, u32[]{:S(2)}) copy-start(f32[256,256]{1,0:T(8,128)} %param.16) | copy-start | bytes 786436
Sparse Core Ops, SparseCore 0:
  114.3 175.0 all-reduce.5
  326.5 70.3 all-reduce.9
  596.4 109.3 all-reduce.7
